TPU v7x, 256 devices: a whole 4x4x8 slice. The times are simulated.
256 devices in a mesh: ctx: 64 (over y_hi, z, x), head: 4 (over y_lo, core).
Axes of the slice: x: 4, y: 4 (y_hi: 2, y_lo: 2; y = y_hi * 2 + y_lo), z: 8, core: 2. Of those that a mesh axis runs over, the one named last changes fastest.
Arguments:
- queries: bfloat16 [32768, 2560], P(('ctx', 'head')), may hold values from -6 to 6
- keys: bfloat16 [32768, 512], P(('ctx', 'head')), may hold values from -6 to 6
- values: bfloat16 [32768, 512], P(('ctx', 'head')), may hold values from -6 to 6
- attn_out: bfloat16 [32768, 2560], P(('ctx', 'head')), may hold values from -6 to 6
- grad_out: bfloat16 [32768, 2560], P(('ctx', 'head')), may hold values from -6 to 6
- log_norm: float32 [20, 32768], P(None, ('ctx', 'head'))
- doc_lengths: int32 [64], replicated, may hold values from 1 to 3072, as said below
Outputs:
- grad_queries: bfloat16 [32768, 2560], P(('ctx', 'head'))
- grad_keys: bfloat16 [32768, 512], P(('ctx', 'head'))
- grad_values: bfloat16 [32768, 512], P(('ctx', 'head'))
Inputs may be any that keep to these rules, and one draw needn't show every extreme that they name: `doc_lengths`: 64 lengths that sum to 32768; the first document has fewer than 512 tokens and the second has 3072.
All inputs are finite; a program needn't handle non-finite values.
Results may differ from a plain program's by a relative error of at most 0.0054.
Values may be sent and summed in bfloat16 or wider, within the bound.
A program may use at most 64 MiB of HBM per device.

v0:
```python
import jax
import jax.numpy as jnp
from jax import lax
from jax.sharding import PartitionSpec as P

HD = 128
SPAN = 6


def shifted(value, axis, steps):
    count = lax.axis_size(axis)
    pairs = [(source, (source + steps) % count) for source in range(count)]
    return lax.ppermute(value, axis, pairs)


def passed_along(value, axis, by):
    count = lax.axis_size(axis)
    pairs = [(i, i + by) for i in range(count) if 0 <= i + by < count]
    return lax.ppermute(value, axis, pairs)


def doc_starts(positions, doc_lengths):
    doc_ends = jnp.cumsum(doc_lengths)
    marked = jnp.where(doc_ends[None, :] <= positions[:, None], doc_ends[None, :], 0)
    return jnp.max(marked, axis=1)


def body(queries, keys, values, attn_out, grad_out, log_norm, doc_lengths):
    head_count = lax.axis_size("head")
    input_rows = queries.shape[0]
    block_rows = input_rows * head_count
    query_heads_all = queries.shape[1] // HD
    local_kv = keys.shape[1] // (head_count * HD)
    local_query = query_heads_all // head_count
    group_size = local_query // local_kv
    softmax_scale = HD ** (-0.5)
    products = (grad_out.astype(jnp.float32) * attn_out.astype(jnp.float32)).reshape(
        input_rows, query_heads_all, HD
    )
    row_delta = jnp.sum(products, axis=2).T
    query_cols, grad_cols, key_cols, value_cols = (
        lax.all_to_all(queries, "head", split_axis=1, concat_axis=0, tiled=True),
        lax.all_to_all(grad_out, "head", split_axis=1, concat_axis=0, tiled=True),
        lax.all_to_all(keys, "head", split_axis=1, concat_axis=0, tiled=True),
        lax.all_to_all(values, "head", split_axis=1, concat_axis=0, tiled=True),
    )
    norm_rows, delta_rows = (
        lax.all_to_all(log_norm, "head", split_axis=0, concat_axis=1, tiled=True),
        lax.all_to_all(row_delta, "head", split_axis=0, concat_axis=1, tiled=True),
    )
    query_heads = query_cols.reshape(block_rows, local_kv, group_size, HD)
    grad_heads = grad_cols.reshape(block_rows, local_kv, group_size, HD)
    key_heads = key_cols.reshape(block_rows, local_kv, HD)
    value_heads = value_cols.reshape(block_rows, local_kv, HD)
    norm_heads = norm_rows.reshape(local_kv, group_size, block_rows)
    delta_heads = delta_rows.reshape(local_kv, group_size, block_rows)
    ctx_count = lax.axis_size("ctx")
    ctx_index = lax.axis_index("ctx")
    row_offset = ctx_index * block_rows
    query_places = row_offset + jnp.arange(block_rows, dtype=jnp.int32)
    row_starts = doc_starts(query_places, doc_lengths)
    last_query = row_offset + block_rows - 1
    first_start = row_starts[0]

    def tile_terms(key_block, value_block, key_first):
        key_count = key_block.shape[0]

        def compute():
            key_places = key_first + jnp.arange(key_count, dtype=jnp.int32)
            allowed = (key_places[None, :] >= row_starts[:, None]) & (
                key_places[None, :] <= query_places[:, None]
            )
            scores = (
                jnp.einsum(
                    "igxd,jgd->gxij", query_heads, key_block, preferred_element_type=jnp.float32
                )
                * softmax_scale
            )
            weights = jnp.where(allowed[None, None], jnp.exp(scores - norm_heads[..., None]), 0.0)
            weight_grads = jnp.einsum(
                "igxd,jgd->gxij", grad_heads, value_block, preferred_element_type=jnp.float32
            )
            score_grads = weights * (weight_grads - delta_heads[..., None])
            weights_low = weights.astype(jnp.bfloat16)
            grads_low = score_grads.astype(jnp.bfloat16)
            grad_query = (
                jnp.einsum(
                    "gxij,jgd->igxd", grads_low, key_block, preferred_element_type=jnp.float32
                )
                * softmax_scale
            )
            grad_key = (
                jnp.einsum(
                    "gxij,igxd->jgd", grads_low, query_heads, preferred_element_type=jnp.float32
                )
                * softmax_scale
            )
            grad_value = jnp.einsum(
                "gxij,igxd->jgd", weights_low, grad_heads, preferred_element_type=jnp.float32
            )
            return (grad_query, grad_key, grad_value)

        def skip():
            return (
                jnp.zeros((block_rows, local_kv, group_size, HD), jnp.float32),
                jnp.zeros((key_count, local_kv, HD), jnp.float32),
                jnp.zeros((key_count, local_kv, HD), jnp.float32),
            )

        live_tile = (key_first <= last_query) & (key_first + key_count - 1 >= first_start)
        return lax.cond(live_tile, compute, skip)

    zero_query = jnp.zeros((block_rows, local_kv, group_size, HD), jnp.float32)
    zero_keys = jnp.zeros((block_rows, local_kv, HD), jnp.float32)

    def visit_turn(turn_index, visit_state):
        key_block, value_block, key_grads, value_grads, query_grads = visit_state
        owner_index = (ctx_index - turn_index) % ctx_count
        grad_query, grad_key, grad_value = tile_terms(
            key_block, value_block, owner_index * block_rows
        )
        key_grads, value_grads = shifted((key_grads + grad_key, value_grads + grad_value), "ctx", 1)
        key_block, value_block = passed_along((key_block, value_block), "ctx", 1)
        return (key_block, value_block, key_grads, value_grads, query_grads + grad_query)

    key_block, value_block, key_grads, value_grads, query_grads = lax.fori_loop(
        0, SPAN, visit_turn, (key_heads, value_heads, zero_keys, zero_keys, zero_query)
    )
    final_owner = (ctx_index - SPAN) % ctx_count
    grad_query, grad_key, grad_value = tile_terms(key_block, value_block, final_owner * block_rows)
    key_total, value_total = (
        shifted((key_grads + grad_key).astype(jnp.bfloat16), "ctx", -SPAN).astype(jnp.float32),
        shifted((value_grads + grad_value).astype(jnp.bfloat16), "ctx", -SPAN).astype(jnp.float32),
    )
    query_total = query_grads + grad_query
    query_result = query_total.astype(jnp.bfloat16).reshape(block_rows, local_query * HD)
    key_result = key_total.astype(jnp.bfloat16).reshape(block_rows, local_kv * HD)
    value_result = value_total.astype(jnp.bfloat16).reshape(block_rows, local_kv * HD)
    return (
        lax.all_to_all(query_result, "head", split_axis=0, concat_axis=1, tiled=True),
        lax.all_to_all(key_result, "head", split_axis=0, concat_axis=1, tiled=True),
        lax.all_to_all(value_result, "head", split_axis=0, concat_axis=1, tiled=True),
    )


def solution(mesh):
    placed = (
        P(("ctx", "head"), None),
        P(("ctx", "head"), None),
        P(("ctx", "head"), None),
        P(("ctx", "head"), None),
        P(("ctx", "head"), None),
        P(None, ("ctx", "head")),
        P(),
    )
    return jax.shard_map(
        body,
        mesh=mesh,
        in_specs=placed,
        out_specs=(P(("ctx", "head"), None), P(("ctx", "head"), None), P(("ctx", "head"), None)),
        check_vma=False,
    )
```

profile of v0, /device:TPU:86, one launch (start us, length us, event | category | flops | bytes accessed | tf_op | source)
XLA Modules:
  0.0 310.9 jit_solution(14211405744093583525)
XLA Ops:
  18.0 7.7 %all_to_all.159 = bf16[128,4,128]{2,0,1:T(8,128)(2,1)} all-to-all(bf16[128,4,128]{2,0,1:T(8,128)(2,1)S(1)} %copy_bitcast_fusion.1), channel_id=1, replica_groups=mesh['ctx'=64,'head'=4] {'head'}, dimensions={1} | all-to-all | bytes 262144 | tf_op jit(solution)/shard_map/all_to_all | solution.py:44
  30.2 9.1 %all-to-all-done.4 = bf16[128,4,640]{0,2,1:T(8,128)(2,1)S(1)} async-done(((bf16[128,4,640]{0,2,1:T(8,128)(2,1)}), bf16[128,4,640]{0,2,1:T(8,128)(2,1)S(1)}, u32[]{:S(2)}, u32[]{:S(2)}) %all-to-all-start.4) | async-done | bytes 655392 | tf_op jit(solution)/shard_map/all_to_all | solution.py:43
  43.9 9.2 %all-to-all-done.2 = bf16[128,4,640]{0,2,1:T(8,128)(2,1)S(1)} async-done(((bf16[128,4,640]{0,2,1:T(8,128)(2,1)}), bf16[128,4,640]{0,2,1:T(8,128)(2,1)S(1)}, u32[]{:S(2)}, u32[]{:S(2)}) %all-to-all-start.2) | async-done | bytes 655392 | tf_op jit(solution)/shard_map/all_to_all | solution.py:42
  53.1 4.0 %all-to-all-start.1 = ((bf16[128,4,128]{2,0,1:T(8,128)(2,1)}), bf16[128,4,128]{2,0,1:T(8,128)(2,1)}, u32[]{:S(2)}, u32[]{:S(2)}) async-start(bf16[128,4,128]{2,0,1:T(8,128)(2,1)} %copy_bitcast_fusion), calls=%async_computation.1 | async-start | bytes 262144 | tf_op jit(solution)/shard_map/all_to_all | solution.py:45
  67.2 190.1 %while.26 = (s32[]{:T(128)}, bf16[512,1,128]{2,0,1:T(8,128)(2,1)}, bf16[512,1,128]{2,0,1:T(8,128)(2,1)}, f32[512,1,128]{2,0,1:T(8,128)}, f32[512,1,128]{2,0,1:T(...) while((s32[]{:T(128)}, bf16[512,1,128]{2,0,1:T(8,128)(2,1)}, ...), condition=%wide.region_6.7_spmd.clone, body=%wide.region_3.6_spmd.clone.sunk | while | flops 1692795904 | bytes 44823308 | solution.py:126
  78.2 8.9 %conditional.5 = (f32[512,1,5,128]{3,0,2,1:T(8,128)S(1)}, f32[512,1,128]{2,0,1:T(8,128)S(1)}, f32[512,1,128]{2,0,1:T(8,128)S(1)}) conditional(s32[]{:T(128)} %convert_element_type.78, () %tuple.89, (s32[]{:T(128)}, s32[512]{0:T(512)S(1)}, s32[]{:T(128)}, bf16[512,1,128]{2,0,1:T(8,128)(2,1)}, bf16[512,1,5,128]{3,0,2,1:T(8,128)(2,1)}, ...), branch_computations={%region_4.4_spmd, %region_5.5_spmd} | conditional | flops 1692009472 | bytes 34597008 | solution.py:111
  92.0 5.2 %collective-permute-done.3 = f32[512,1,128]{2,0,1:T(8,128)S(1)} collective-permute-done((f32[512,1,128]{2,0,1:T(8,128)}, f32[512,1,128]{2,0,1:T(8,128)S(1)}, u32[]{:S(2)}, u32[]{:S(2)}) %collective-permute-start.3) | collective-permute-done | bytes 262176 | tf_op jit(solution)/shard_map/while/body/eval_jaxpr/ppermute | solution.py:13
  97.2 4.5 %collective-permute-done.2 = f32[512,1,128]{2,0,1:T(8,128)S(1)} collective-permute-done((f32[512,1,128]{2,0,1:T(8,128)S(1)}, f32[512,1,128]{2,0,1:T(8,128)S(1)}, u32[]{:S(2)}, u32[]{:S(2)}) %collective-permute-start.2) | collective-permute-done | bytes 262176 | tf_op jit(solution)/shard_map/while/body/eval_jaxpr/ppermute | solution.py:13
  104.0 5.5 %collective-permute-start = (bf16[512,1,128]{2,0,1:T(8,128)(2,1)}, bf16[512,1,128]{2,0,1:T(8,128)(2,1)}, u32[]{:S(2)}, u32[]{:S(2)}) collective-permute-start(bf16[512,1,128]{2,0,1:T(8,128)(2,1)} %copy.133), channel_id=1, source_target_pairs={{0,4},{4,8},{8,12},{12,16},{16,20},{20,24},{24,28},{28,32},{32,36}... | collective-permute-start | bytes 393224 | tf_op jit(solution)/shard_map/while/body/eval_jaxpr/ppermute | solution.py:19
  113.8 8.9 %conditional.5 = (f32[512,1,5,128]{3,0,2,1:T(8,128)S(1)}, f32[512,1,128]{2,0,1:T(8,128)S(1)}, f32[512,1,128]{2,0,1:T(8,128)S(1)}) conditional(s32[]{:T(128)} %convert_element_type.78, () %tuple.89, (s32[]{:T(128)}, s32[512]{0:T(512)S(1)}, s32[]{:T(128)}, bf16[512,1,128]{2,0,1:T(8,128)(2,1)}, bf16[512,1,5,128]{3,0,2,1:T(8,128)(2,1)}, ...), branch_computations={%region_4.4_spmd, %region_5.5_spmd} | conditional | flops 1692009472 | bytes 34597008 | solution.py:111
  128.5 4.4 %collective-permute-done.3 = f32[512,1,128]{2,0,1:T(8,128)S(1)} collective-permute-done((f32[512,1,128]{2,0,1:T(8,128)}, f32[512,1,128]{2,0,1:T(8,128)S(1)}, u32[]{:S(2)}, u32[]{:S(2)}) %collective-permute-start.3) | collective-permute-done | bytes 262176 | tf_op jit(solution)/shard_map/while/body/eval_jaxpr/ppermute | solution.py:13
  138.5 5.8 %collective-permute-start = (bf16[512,1,128]{2,0,1:T(8,128)(2,1)}, bf16[512,1,128]{2,0,1:T(8,128)(2,1)}, u32[]{:S(2)}, u32[]{:S(2)}) collective-permute-start(bf16[512,1,128]{2,0,1:T(8,128)(2,1)} %copy.133), channel_id=1, source_target_pairs={{0,4},{4,8},{8,12},{12,16},{16,20},{20,24},{24,28},{28,32},{32,36}... | collective-permute-start | bytes 393224 | tf_op jit(solution)/shard_map/while/body/eval_jaxpr/ppermute | solution.py:19
  154.6 9.1 %collective-permute-start.2 = (f32[512,1,128]{2,0,1:T(8,128)S(1)}, f32[512,1,128]{2,0,1:T(8,128)S(1)}, u32[]{:S(2)}, u32[]{:S(2)}) collective-permute-start(f32[512,1,128]{2,0,1:T(8,128)S(1)} %add.190), channel_id=1, source_target_pairs={{0,4},{4,8},{8,12},{12,16},{16,20},{20,24},{24,28},{28,32},{32,36}... | collective-permute-start | bytes 786440 | tf_op jit(solution)/shard_map/while/body/eval_jaxpr/ppermute | solution.py:13
  169.9 6.7 %collective-permute-start = (bf16[512,1,128]{2,0,1:T(8,128)(2,1)}, bf16[512,1,128]{2,0,1:T(8,128)(2,1)}, u32[]{:S(2)}, u32[]{:S(2)}) collective-permute-start(bf16[512,1,128]{2,0,1:T(8,128)(2,1)} %copy.133), channel_id=1, source_target_pairs={{0,4},{4,8},{8,12},{12,16},{16,20},{20,24},{24,28},{28,32},{32,36}... | collective-permute-start | bytes 393224 | tf_op jit(solution)/shard_map/while/body/eval_jaxpr/ppermute | solution.py:19
  178.1 4.9 %collective-permute-start.1 = (bf16[512,1,128]{2,0,1:T(8,128)(2,1)}, bf16[512,1,128]{2,0,1:T(8,128)(2,1)}, u32[]{:S(2)}, u32[]{:S(2)}) collective-permute-start(bf16[512,1,128]{2,0,1:T(8,128)(2,1)} %copy.134), channel_id=1, source_target_pairs={{0,4},{4,8},{8,12},{12,16},{16,20},{20,24},{24,28},{28,32},{32,36}... | collective-permute-start | bytes 393224 | tf_op jit(solution)/shard_map/while/body/eval_jaxpr/ppermute | solution.py:19
  188.9 4.7 %collective-permute-done.3 = f32[512,1,128]{2,0,1:T(8,128)S(1)} collective-permute-done((f32[512,1,128]{2,0,1:T(8,128)}, f32[512,1,128]{2,0,1:T(8,128)S(1)}, u32[]{:S(2)}, u32[]{:S(2)}) %collective-permute-start.3) | collective-permute-done | bytes 262176 | tf_op jit(solution)/shard_map/while/body/eval_jaxpr/ppermute | solution.py:13
  198.7 10.2 %collective-permute-start = (bf16[512,1,128]{2,0,1:T(8,128)(2,1)}, bf16[512,1,128]{2,0,1:T(8,128)(2,1)}, u32[]{:S(2)}, u32[]{:S(2)}) collective-permute-start(bf16[512,1,128]{2,0,1:T(8,128)(2,1)} %copy.133), channel_id=1, source_target_pairs={{0,4},{4,8},{8,12},{12,16},{16,20},{20,24},{24,28},{28,32},{32,36}... | collective-permute-start | bytes 393224 | tf_op jit(solution)/shard_map/while/body/eval_jaxpr/ppermute | solution.py:19
  210.5 5.1 %collective-permute-start.1 = (bf16[512,1,128]{2,0,1:T(8,128)(2,1)}, bf16[512,1,128]{2,0,1:T(8,128)(2,1)}, u32[]{:S(2)}, u32[]{:S(2)}) collective-permute-start(bf16[512,1,128]{2,0,1:T(8,128)(2,1)} %copy.134), channel_id=1, source_target_pairs={{0,4},{4,8},{8,12},{12,16},{16,20},{20,24},{24,28},{28,32},{32,36}... | collective-permute-start | bytes 393224 | tf_op jit(solution)/shard_map/while/body/eval_jaxpr/ppermute | solution.py:19
  230.1 6.5 %collective-permute-start = (bf16[512,1,128]{2,0,1:T(8,128)(2,1)}, bf16[512,1,128]{2,0,1:T(8,128)(2,1)}, u32[]{:S(2)}, u32[]{:S(2)}) collective-permute-start(bf16[512,1,128]{2,0,1:T(8,128)(2,1)} %copy.133), channel_id=1, source_target_pairs={{0,4},{4,8},{8,12},{12,16},{16,20},{20,24},{24,28},{28,32},{32,36}... | collective-permute-start | bytes 393224 | tf_op jit(solution)/shard_map/while/body/eval_jaxpr/ppermute | solution.py:19
  238.2 6.8 %collective-permute-start.1 = (bf16[512,1,128]{2,0,1:T(8,128)(2,1)}, bf16[512,1,128]{2,0,1:T(8,128)(2,1)}, u32[]{:S(2)}, u32[]{:S(2)}) collective-permute-start(bf16[512,1,128]{2,0,1:T(8,128)(2,1)} %copy.134), channel_id=1, source_target_pairs={{0,4},{4,8},{8,12},{12,16},{16,20},{20,24},{24,28},{28,32},{32,36}... | collective-permute-start | bytes 393224 | tf_op jit(solution)/shard_map/while/body/eval_jaxpr/ppermute | solution.py:19
  261.3 7.5 %collective-permute-start.5 = (bf16[512,1,128]{2,0,1:T(8,128)(2,1)S(1)}, bf16[512,1,128]{2,0,1:T(8,128)(2,1)}, u32[]{:S(2)}, u32[]{:S(2)}) collective-permute-start(bf16[512,1,128]{2,0,1:T(8,128)(2,1)S(1)} %add_convert_fusion.1), channel_id=1, source_target_pairs={{0,232},{4,236},{8,240},{12,244},{16,248},{20,252},{24,0},{28,4},{... | collective-permute-start | bytes 393224 | tf_op jit(solution)/shard_map/ppermute | solution.py:13
  268.9 11.4 %collective-permute-done.4 = bf16[512,1,128]{2,0,1:T(8,128)(2,1)} collective-permute-done((bf16[512,1,128]{2,0,1:T(8,128)(2,1)S(1)}, bf16[512,1,128]{2,0,1:T(8,128)(2,1)}, u32[]{:S(2)}, u32[]{:S(2)}) %collective-permute-start.4) | collective-permute-done | bytes 131104 | tf_op jit(solution)/shard_map/ppermute | solution.py:13
  283.6 4.6 %all-to-all-done.7 = bf16[4,128,128]{2,1,0:T(8,128)(2,1)S(1)} async-done(((bf16[4,128,128]{2,1,0:T(8,128)(2,1)}), bf16[4,128,128]{2,1,0:T(8,128)(2,1)S(1)}, u32[]{:S(2)}, u32[]{:S(2)}) %all-to-all-start.7) | async-done | bytes 131104 | tf_op jit(solution)/shard_map/all_to_all | solution.py:141
  301.5 8.4 %all-to-all-done.6 = bf16[4,128,640]{1,2,0:T(8,128)(2,1)S(1)} async-done(((bf16[4,128,640]{1,2,0:T(8,128)(2,1)}), bf16[4,128,640]{1,2,0:T(8,128)(2,1)S(1)}, u32[]{:S(2)}, u32[]{:S(2)}) %all-to-all-start.6) | async-done | bytes 655392 | tf_op jit(solution)/shard_map/all_to_all | solution.py:140
  (199 shorter events, 163.6 us)
Async XLA Ops:
  25.7 13.7 %all-to-all-start.4 = ((bf16[128,4,640]{0,2,1:T(8,128)(2,1)}), bf16[128,4,640]{0,2,1:T(8,128)(2,1)S(1)}, u32[]{:S(2)}, u32[]{:S(2)}) async-start(bf16[128,4,640]{0,2,1:T(8,128)(2,1)} %bitcast.56), calls=%async_computation.4 | async-start | bytes 1310720 | tf_op jit(solution)/shard_map/all_to_all | solution.py:43
  39.4 13.7 %all-to-all-start.2 = ((bf16[128,4,640]{0,2,1:T(8,128)(2,1)}), bf16[128,4,640]{0,2,1:T(8,128)(2,1)S(1)}, u32[]{:S(2)}, u32[]{:S(2)}) async-start(bf16[128,4,640]{0,2,1:T(8,128)(2,1)} %bitcast.52), calls=%async_computation.2 | async-start | bytes 1310720 | tf_op jit(solution)/shard_map/all_to_all | solution.py:42
  53.1 13.4 %all-to-all-start.1 = ((bf16[128,4,128]{2,0,1:T(8,128)(2,1)}), bf16[128,4,128]{2,0,1:T(8,128)(2,1)}, u32[]{:S(2)}, u32[]{:S(2)}) async-start(bf16[128,4,128]{2,0,1:T(8,128)(2,1)} %copy_bitcast_fusion), calls=%async_computation.1 | async-start | bytes 262144 | tf_op jit(solution)/shard_map/all_to_all | solution.py:45
  68.8 23.2 %collective-permute-start = (bf16[512,1,128]{2,0,1:T(8,128)(2,1)}, bf16[512,1,128]{2,0,1:T(8,128)(2,1)}, u32[]{:S(2)}, u32[]{:S(2)}) collective-permute-start(bf16[512,1,128]{2,0,1:T(8,128)(2,1)} %copy.133), channel_id=1, source_target_pairs={{0,4},{4,8},{8,12},{12,16},{16,20},{20,24},{24,28},{28,32},{32,36}... | collective-permute-start | bytes 393224 | tf_op jit(solution)/shard_map/while/body/eval_jaxpr/ppermute | solution.py:19
  74.1 17.9 %collective-permute-start.1 = (bf16[512,1,128]{2,0,1:T(8,128)(2,1)}, bf16[512,1,128]{2,0,1:T(8,128)(2,1)}, u32[]{:S(2)}, u32[]{:S(2)}) collective-permute-start(bf16[512,1,128]{2,0,1:T(8,128)(2,1)} %copy.134), channel_id=1, source_target_pairs={{0,4},{4,8},{8,12},{12,16},{16,20},{20,24},{24,28},{28,32},{32,36}... | collective-permute-start | bytes 393224 | tf_op jit(solution)/shard_map/while/body/eval_jaxpr/ppermute | solution.py:19
  87.8 9.4 %collective-permute-start.3 = (f32[512,1,128]{2,0,1:T(8,128)}, f32[512,1,128]{2,0,1:T(8,128)S(1)}, u32[]{:S(2)}, u32[]{:S(2)}) collective-permute-start(f32[512,1,128]{2,0,1:T(8,128)} %add.191), channel_id=1, source_target_pairs={{0,4},{4,8},{8,12},{12,16},{16,20},{20,24},{24,28},{28,32},{32,36}... | collective-permute-start | bytes 786440 | tf_op jit(solution)/shard_map/while/body/eval_jaxpr/ppermute | solution.py:13
  90.3 11.5 %collective-permute-start.2 = (f32[512,1,128]{2,0,1:T(8,128)S(1)}, f32[512,1,128]{2,0,1:T(8,128)S(1)}, u32[]{:S(2)}, u32[]{:S(2)}) collective-permute-start(f32[512,1,128]{2,0,1:T(8,128)S(1)} %add.190), channel_id=1, source_target_pairs={{0,4},{4,8},{8,12},{12,16},{16,20},{20,24},{24,28},{28,32},{32,36}... | collective-permute-start | bytes 786440 | tf_op jit(solution)/shard_map/while/body/eval_jaxpr/ppermute | solution.py:13
  104.0 24.4 %collective-permute-start = (bf16[512,1,128]{2,0,1:T(8,128)(2,1)}, bf16[512,1,128]{2,0,1:T(8,128)(2,1)}, u32[]{:S(2)}, u32[]{:S(2)}) collective-permute-start(bf16[512,1,128]{2,0,1:T(8,128)(2,1)} %copy.133), channel_id=1, source_target_pairs={{0,4},{4,8},{8,12},{12,16},{16,20},{20,24},{24,28},{28,32},{32,36}... | collective-permute-start | bytes 393224 | tf_op jit(solution)/shard_map/while/body/eval_jaxpr/ppermute | solution.py:19
  111.1 17.4 %collective-permute-start.1 = (bf16[512,1,128]{2,0,1:T(8,128)(2,1)}, bf16[512,1,128]{2,0,1:T(8,128)(2,1)}, u32[]{:S(2)}, u32[]{:S(2)}) collective-permute-start(bf16[512,1,128]{2,0,1:T(8,128)(2,1)} %copy.134), channel_id=1, source_target_pairs={{0,4},{4,8},{8,12},{12,16},{16,20},{20,24},{24,28},{28,32},{32,36}... | collective-permute-start | bytes 393224 | tf_op jit(solution)/shard_map/while/body/eval_jaxpr/ppermute | solution.py:19
  123.4 9.5 %collective-permute-start.3 = (f32[512,1,128]{2,0,1:T(8,128)}, f32[512,1,128]{2,0,1:T(8,128)S(1)}, u32[]{:S(2)}, u32[]{:S(2)}) collective-permute-start(f32[512,1,128]{2,0,1:T(8,128)} %add.191), channel_id=1, source_target_pairs={{0,4},{4,8},{8,12},{12,16},{16,20},{20,24},{24,28},{28,32},{32,36}... | collective-permute-start | bytes 786440 | tf_op jit(solution)/shard_map/while/body/eval_jaxpr/ppermute | solution.py:13
  126.5 9.7 %collective-permute-start.2 = (f32[512,1,128]{2,0,1:T(8,128)S(1)}, f32[512,1,128]{2,0,1:T(8,128)S(1)}, u32[]{:S(2)}, u32[]{:S(2)}) collective-permute-start(f32[512,1,128]{2,0,1:T(8,128)S(1)} %add.190), channel_id=1, source_target_pairs={{0,4},{4,8},{8,12},{12,16},{16,20},{20,24},{24,28},{28,32},{32,36}... | collective-permute-start | bytes 786440 | tf_op jit(solution)/shard_map/while/body/eval_jaxpr/ppermute | solution.py:13
  138.5 25.6 %collective-permute-start = (bf16[512,1,128]{2,0,1:T(8,128)(2,1)}, bf16[512,1,128]{2,0,1:T(8,128)(2,1)}, u32[]{:S(2)}, u32[]{:S(2)}) collective-permute-start(bf16[512,1,128]{2,0,1:T(8,128)(2,1)} %copy.133), channel_id=1, source_target_pairs={{0,4},{4,8},{8,12},{12,16},{16,20},{20,24},{24,28},{28,32},{32,36}... | collective-permute-start | bytes 393224 | tf_op jit(solution)/shard_map/while/body/eval_jaxpr/ppermute | solution.py:19
  145.9 18.2 %collective-permute-start.1 = (bf16[512,1,128]{2,0,1:T(8,128)(2,1)}, bf16[512,1,128]{2,0,1:T(8,128)(2,1)}, u32[]{:S(2)}, u32[]{:S(2)}) collective-permute-start(bf16[512,1,128]{2,0,1:T(8,128)(2,1)} %copy.134), channel_id=1, source_target_pairs={{0,4},{4,8},{8,12},{12,16},{16,20},{20,24},{24,28},{28,32},{32,36}... | collective-permute-start | bytes 393224 | tf_op jit(solution)/shard_map/while/body/eval_jaxpr/ppermute | solution.py:19
  151.1 13.0 %collective-permute-start.3 = (f32[512,1,128]{2,0,1:T(8,128)}, f32[512,1,128]{2,0,1:T(8,128)S(1)}, u32[]{:S(2)}, u32[]{:S(2)}) collective-permute-start(f32[512,1,128]{2,0,1:T(8,128)} %add.191), channel_id=1, source_target_pairs={{0,4},{4,8},{8,12},{12,16},{16,20},{20,24},{24,28},{28,32},{32,36}... | collective-permute-start | bytes 786440 | tf_op jit(solution)/shard_map/while/body/eval_jaxpr/ppermute | solution.py:13
  154.6 13.0 %collective-permute-start.2 = (f32[512,1,128]{2,0,1:T(8,128)S(1)}, f32[512,1,128]{2,0,1:T(8,128)S(1)}, u32[]{:S(2)}, u32[]{:S(2)}) collective-permute-start(f32[512,1,128]{2,0,1:T(8,128)S(1)} %add.190), channel_id=1, source_target_pairs={{0,4},{4,8},{8,12},{12,16},{16,20},{20,24},{24,28},{28,32},{32,36}... | collective-permute-start | bytes 786440 | tf_op jit(solution)/shard_map/while/body/eval_jaxpr/ppermute | solution.py:13
  169.9 19.0 %collective-permute-start = (bf16[512,1,128]{2,0,1:T(8,128)(2,1)}, bf16[512,1,128]{2,0,1:T(8,128)(2,1)}, u32[]{:S(2)}, u32[]{:S(2)}) collective-permute-start(bf16[512,1,128]{2,0,1:T(8,128)(2,1)} %copy.133), channel_id=1, source_target_pairs={{0,4},{4,8},{8,12},{12,16},{16,20},{20,24},{24,28},{28,32},{32,36}... | collective-permute-start | bytes 393224 | tf_op jit(solution)/shard_map/while/body/eval_jaxpr/ppermute | solution.py:19
  178.1 10.8 %collective-permute-start.1 = (bf16[512,1,128]{2,0,1:T(8,128)(2,1)}, bf16[512,1,128]{2,0,1:T(8,128)(2,1)}, u32[]{:S(2)}, u32[]{:S(2)}) collective-permute-start(bf16[512,1,128]{2,0,1:T(8,128)(2,1)} %copy.134), channel_id=1, source_target_pairs={{0,4},{4,8},{8,12},{12,16},{16,20},{20,24},{24,28},{28,32},{32,36}... | collective-permute-start | bytes 393224 | tf_op jit(solution)/shard_map/while/body/eval_jaxpr/ppermute | solution.py:19
  198.7 22.7 %collective-permute-start = (bf16[512,1,128]{2,0,1:T(8,128)(2,1)}, bf16[512,1,128]{2,0,1:T(8,128)(2,1)}, u32[]{:S(2)}, u32[]{:S(2)}) collective-permute-start(bf16[512,1,128]{2,0,1:T(8,128)(2,1)} %copy.133), channel_id=1, source_target_pairs={{0,4},{4,8},{8,12},{12,16},{16,20},{20,24},{24,28},{28,32},{32,36}... | collective-permute-start | bytes 393224 | tf_op jit(solution)/shard_map/while/body/eval_jaxpr/ppermute | solution.py:19
  210.5 11.0 %collective-permute-start.1 = (bf16[512,1,128]{2,0,1:T(8,128)(2,1)}, bf16[512,1,128]{2,0,1:T(8,128)(2,1)}, u32[]{:S(2)}, u32[]{:S(2)}) collective-permute-start(bf16[512,1,128]{2,0,1:T(8,128)(2,1)} %copy.134), channel_id=1, source_target_pairs={{0,4},{4,8},{8,12},{12,16},{16,20},{20,24},{24,28},{28,32},{32,36}... | collective-permute-start | bytes 393224 | tf_op jit(solution)/shard_map/while/body/eval_jaxpr/ppermute | solution.py:19
  230.1 23.0 %collective-permute-start = (bf16[512,1,128]{2,0,1:T(8,128)(2,1)}, bf16[512,1,128]{2,0,1:T(8,128)(2,1)}, u32[]{:S(2)}, u32[]{:S(2)}) collective-permute-start(bf16[512,1,128]{2,0,1:T(8,128)(2,1)} %copy.133), channel_id=1, source_target_pairs={{0,4},{4,8},{8,12},{12,16},{16,20},{20,24},{24,28},{28,32},{32,36}... | collective-permute-start | bytes 393224 | tf_op jit(solution)/shard_map/while/body/eval_jaxpr/ppermute | solution.py:19
  238.2 15.0 %collective-permute-start.1 = (bf16[512,1,128]{2,0,1:T(8,128)(2,1)}, bf16[512,1,128]{2,0,1:T(8,128)(2,1)}, u32[]{:S(2)}, u32[]{:S(2)}) collective-permute-start(bf16[512,1,128]{2,0,1:T(8,128)(2,1)} %copy.134), channel_id=1, source_target_pairs={{0,4},{4,8},{8,12},{12,16},{16,20},{20,24},{24,28},{28,32},{32,36}... | collective-permute-start | bytes 393224 | tf_op jit(solution)/shard_map/while/body/eval_jaxpr/ppermute | solution.py:19
  258.3 22.0 %collective-permute-start.4 = (bf16[512,1,128]{2,0,1:T(8,128)(2,1)S(1)}, bf16[512,1,128]{2,0,1:T(8,128)(2,1)}, u32[]{:S(2)}, u32[]{:S(2)}) collective-permute-start(bf16[512,1,128]{2,0,1:T(8,128)(2,1)S(1)} %add_convert_fusion.2), channel_id=1, source_target_pairs={{0,232},{4,236},{8,240},{12,244},{16,248},{20,252},{24,0},{28,4},{... | collective-permute-start | bytes 393224 | tf_op jit(solution)/shard_map/ppermute | solution.py:13
  261.3 22.3 %collective-permute-start.5 = (bf16[512,1,128]{2,0,1:T(8,128)(2,1)S(1)}, bf16[512,1,128]{2,0,1:T(8,128)(2,1)}, u32[]{:S(2)}, u32[]{:S(2)}) collective-permute-start(bf16[512,1,128]{2,0,1:T(8,128)(2,1)S(1)} %add_convert_fusion.1), channel_id=1, source_target_pairs={{0,232},{4,236},{8,240},{12,244},{16,248},{20,252},{24,0},{28,4},{... | collective-permute-start | bytes 393224 | tf_op jit(solution)/shard_map/ppermute | solution.py:13
  296.2 13.7 %all-to-all-start.6 = ((bf16[4,128,640]{1,2,0:T(8,128)(2,1)}), bf16[4,128,640]{1,2,0:T(8,128)(2,1)S(1)}, u32[]{:S(2)}, u32[]{:S(2)}) async-start(bf16[4,128,640]{1,2,0:T(8,128)(2,1)} %copy.108), calls=%async_computation.6 | async-start | bytes 1310720 | tf_op jit(solution)/shard_map/all_to_all | solution.py:140
  (33 other events, 292.3 us)
where the time goes:
time: 313 us; the launch traced here: 311 us
  starting transfers between devices  131 us (42%)
  waiting for transfers between devices  86.1 us (28%)
  local copies, waits for them, and re-layouts  46.4 us (15%)
  matrix products  17 us (5%)
  other arithmetic  15.8 us (5%)
  blocking collectives  7.68 us (2%)
  loops' own time  5.29 us (2%)
    ppermute x12, starting transfers between devices, passed_along(): return lax.ppermute(value, axis, pairs)  64.2 us
    ppermute x14, waiting for transfers between devices, shifted(): return lax.ppermute(value, axis, pairs)  49.8 us
    ppermute x14, starting transfers between devices, shifted(): return lax.ppermute(value, axis, pairs)  39.4 us
    while x24, local copies, waits for them, and re-layouts  23 us
    unnamed x26, local copies, waits for them, and re-layouts  10.1 us
    all_to_all x1, waiting for transfers between devices, body(): lax.all_to_all(queries, 'head', split_axis=1, concat_axis=0, tiled=True)  9.15 us
    all_to_all x1, waiting for transfers between devices, body(): lax.all_to_all(grad_out, 'head', split_axis=1, concat_axis=0, tiled=True)  9.13 us
    all_to_all x1, waiting for transfers between devices, body(): lax.all_to_all(query_result, 'head', split_axis=0, concat_axis=1, tiled=T...  8.4 us
  transfers between devices with their start and end apart: 34, of which 18 were waited for; matrix products, arithmetic and copies ran while one was open for 20% of the time, Pallas kernels for 0%

commit v1 on v0

v1 whole, which is shorter than its diff:
```python
import functools

import jax
import jax.numpy as jnp
from jax import lax
from jax.experimental import pallas as pl
from jax.experimental.pallas import tpu as pltpu
from jax.sharding import PartitionSpec as P

HD = 128
ROW = 4
BACK = 3
FAR = 1e30
MESH = pl.DeviceIdType.MESH


class Parts:
    def __init__(self, copies, whole, out_sem):
        self.copies, self.whole, self.out_sem = copies, whole, out_sem

    def start(self):
        for copy in self.copies:
            copy.start()

    def wait_send(self):
        pltpu.make_async_copy(self.whole, self.whole, self.out_sem).wait()


def kernel(
    planes,
    group,
    docs_ref,
    q_ref,
    k_ref,
    v_ref,
    o_ref,
    do_ref,
    norm_ref,
    dq_ref,
    dk_ref,
    dv_ref,
    o_vm,
    do_vm,
    qd_buf,
    relay_buf,
    qt_buf,
    kv_buf,
    kt_buf,
    stat_send,
    stat_recv,
    doc_rows,
    key_marks,
    acc_kv,
    acc_q,
    grad_send,
    core_recv,
    y_recv,
    z_recv,
    dq_send,
    dkv_send,
    local_sem,
    q_sem,
    q_out_sem,
    relay_sem,
    kv_sem,
    kv_in_out_sem,
    kv_out_sem,
    stat_sem,
    core_sem,
    y_sem,
    z_sem,
    grad_out_sem,
    result_sem,
    result_out_sem,
):
    rows = q_ref.shape[0]
    wide = 2 * rows
    unit = 2 * wide
    scale = HD ** (-0.5)
    batches = ((0, 2), (2, group))
    me = lax.axis_index("head")
    ctx = lax.axis_index("ctx")
    side, core = lax.div(me, 2), lax.rem(me, 2)
    plane, place = lax.div(ctx, ROW), lax.rem(ctx, ROW)
    half_plane = 2 * plane + core
    first_core, second_core = core == 0, core == 1
    has_before, has_after = plane >= 1, plane + 1 < planes
    to_core = lax.div(place, 2)
    stays = to_core == core
    my_slot = 2 * lax.rem(place, 2) + core

    core_twin = (ctx, 2 * side + 1 - core)
    side_twin = (ctx, 2 * (1 - side) + core)
    after_same, after_other = (ctx + ROW, me), (ctx + ROW, core_twin[1])
    before_same, before_other = (ctx - ROW, me), (ctx - ROW, core_twin[1])

    def columns(first, count=HD):
        if isinstance(first, int):
            return pl.ds(first, count)
        return pl.ds(pl.multiple_of(first, HD), count)

    def piece_rows(slot):
        return pl.ds(pl.multiple_of(slot * rows, rows), rows)

    def remote(src, dst, out_sem, in_sem, device):
        return pltpu.make_async_remote_copy(
            src_ref=src,
            dst_ref=dst,
            send_sem=out_sem,
            recv_sem=in_sem,
            device_id=device,
            device_id_type=MESH,
        )

    def arrived(ref, sem):
        pltpu.make_async_copy(ref, ref, sem).wait()

    load_o = pltpu.make_async_copy(o_ref, o_vm, local_sem.at[0])
    load_do = pltpu.make_async_copy(do_ref, do_vm, local_sem.at[1])
    load_o.start()
    load_do.start()

    barrier = pltpu.get_barrier_semaphore()

    def greet(device):
        pl.semaphore_signal(barrier, inc=1, device_id=device, device_id_type=MESH)

    for step in range(1, 2 * ROW):
        other = lax.rem(2 * place + core + step, 2 * ROW)
        greet((ROW * plane + lax.div(other, 2), 2 * side + lax.rem(other, 2)))
    greet(side_twin)

    @pl.when(has_after)
    def _():
        greet(after_same)

        @pl.when(second_core)
        def _():
            greet(after_other)

    @pl.when(has_before)
    def _():
        greet(before_same)

        @pl.when(first_core)
        def _():
            greet(before_other)

    pl.semaphore_wait(
        barrier,
        2 * ROW
        + jnp.minimum(planes - 1 - plane, 1) * (1 + core)
        + jnp.minimum(plane, 1) * (2 - core),
    )

    def spread(pairs, out_sem, in_sem, steps=(2, 1, 3)):
        for src, dst in pairs(place):

            @pl.when(stays)
            def _():
                pltpu.make_async_copy(src, dst, in_sem).start()

            @pl.when(jnp.logical_not(stays))
            def _():
                remote(src, dst, out_sem, in_sem, core_twin).start()

        for step in steps:
            other = lax.rem(place + step, ROW)
            for src, dst in pairs(other):
                remote(
                    src, dst, out_sem, in_sem, (ROW * plane + other, 2 * side + to_core)
                ).start()

    for part, ref in ((0, k_ref), (1, v_ref)):
        spread(
            lambda which: [
                (ref.at[:, columns(which * HD)], kv_buf.at[0, 0, part, piece_rows(my_slot), :])
            ],
            kv_in_out_sem.at[0],
            kv_sem.at[0, 0, part],
        )

    after, across, between = (lax.rem(place + step, ROW) for step in (1, 2, 3))
    whole_group = group * HD
    to_between = []
    for index, (x, end) in enumerate(batches):
        to_between.append(
            remote(
                do_ref.at[:, columns(across * whole_group + x * HD, (end - x) * HD)],
                relay_buf.at[:, x * HD : end * HD],
                relay_sem.at[0, index],
                relay_sem.at[1, index],
                (ROW * plane + between, me),
            )
        )
    for index, (x, end) in enumerate(batches):
        to_between[index].start()
        for part, ref, steps in ((0, q_ref, (2, 1, 3)), (1, do_ref, (1, 3))):

            def head_pairs(which):
                cols = columns((which * group + x) * HD, (end - x) * HD)
                return [(ref.at[:, cols], qd_buf.at[part, piece_rows(my_slot), x * HD : end * HD])]

            spread(head_pairs, q_out_sem.at[part], q_sem.at[index], steps)

    load_o.wait()
    load_do.wait()

    def delta_step(which, carry):
        for x in range(group):
            cols = columns((which * group + x) * HD)
            products = do_vm[:, cols].astype(jnp.float32) * o_vm[:, cols].astype(jnp.float32)
            stat_send[which, pl.ds(8 + x, 1), :] = jnp.sum(products.T, axis=0, keepdims=True)
        return carry

    lax.fori_loop(0, ROW, delta_step, 0)
    for which in range(ROW):
        stat_send[which, 0:group, :] = norm_ref[which * group : (which + 1) * group, :]
    spread(
        lambda which: [(stat_send.at[which], stat_recv.at[my_slot])],
        stat_sem.at[0],
        stat_sem.at[1],
    )

    def pass_on(source, target, out, device):
        copies = [
            remote(
                kv_buf.at[source[0], source[1], part],
                kv_buf.at[target[0], target[1], part],
                kv_out_sem.at[out],
                kv_sem.at[target[0], target[1], part],
                device,
            )
            for part in range(2)
        ]
        return Parts(copies, kv_buf.at[0, 0], kv_out_sem.at[out])

    own_to_side = pass_on((0, 0), (0, 1), 0, side_twin)
    own_to_after = pass_on((0, 0), (2, 0), 1, after_same)
    own_to_core = pass_on((0, 0), (1, 0), 2, core_twin)
    side_to_core = pass_on((0, 1), (1, 1), 3, core_twin)
    before_to_side = pass_on((2, 0), (2, 1), 4, side_twin)
    to_second = (3 - 2 * core, 0)
    before_to_core = pass_on((2, 0), to_second, 5, core_twin)
    before_to_after = pass_on((2, 0), (3, 0), 6, after_other)
    to_second_side = (3 - 2 * core, 1)
    before_side_to_core = pass_on((2, 1), to_second_side, 7, core_twin)
    far_to_side = pass_on((3, 0), (3, 1), 8, side_twin)

    def has(k):
        return half_plane >= k

    def wait_kv(k, other, *sends):
        for part in range(2):
            arrived(kv_buf.at[k, other, part], kv_sem.at[k, other, part])
            for condition, send in sends:
                if condition is None:
                    send.copies[part].start()
                else:
                    pl.when(condition)(send.copies[part].start)
        kt_buf[k, other] = kv_buf[k, other, 0].T

    wait_kv(0, 0, (has_after, own_to_after), (None, own_to_side), (first_core, own_to_core))

    acc_kv[...] = jnp.zeros_like(acc_kv)
    acc_q[...] = jnp.zeros_like(acc_q)
    column = lax.broadcasted_iota(jnp.int32, (1, unit), 1)
    places = half_plane * (2 * unit) + side * wide + column + jnp.where(column >= wide, wide, 0)

    def hand_on(index):
        x, end = batches[index]
        arrived(relay_buf.at[:, x * HD : end * HD], relay_sem.at[1, index])
        remote(
            relay_buf.at[:, x * HD : end * HD],
            qd_buf.at[1, piece_rows(2 * lax.rem(after, 2) + core), x * HD : end * HD],
            relay_sem.at[2, index],
            q_sem.at[index],
            (ROW * plane + between, 2 * side + lax.div(after, 2)),
        ).start()

    docs = docs_ref.shape[0]
    lane = lax.broadcasted_iota(jnp.int32, (1, HD), 1)
    doc_rows[...] = jnp.zeros_like(doc_rows)

    def doc_step(index, state):
        first, firsts, ends = state
        end = first + docs_ref[index]
        inside = (places >= first) & (places < end)
        doc_rows[pl.ds(index, 1), :] = jnp.where(inside, 0.0, -FAR)
        here = lane == index
        return end, jnp.where(here, first, firsts), jnp.where(here, end, ends)

    nothing = jnp.zeros((1, HD), jnp.int32)
    unused, doc_firsts, doc_ends = lax.fori_loop(
        0, docs, doc_step, (jnp.int32(0), nothing, nothing)
    )
    hand_on(0)
    query_marks = doc_rows[...].astype(jnp.bfloat16)
    for k in range(BACK + 1):
        for other in range(2):
            row = lax.broadcasted_iota(jnp.int32, (unit, HD), 0)
            row = row + jnp.where(row >= wide, wide, 0)
            key_side = side + other * (1 - 2 * side)
            row = row + ((half_plane - k) * (2 * unit) + key_side * wide)
            lanes = lax.broadcasted_iota(jnp.int32, (unit, HD), 1)
            mark = ((row >= doc_firsts) & (row < doc_ends)) | ((lanes >= docs) & (lanes < docs + 3))
            key_marks[k, other] = jnp.where(mark, 1.0, 0.0).astype(jnp.bfloat16)

    arrived(stat_recv, stat_sem.at[1])

    def three_parts(value):
        high = value.astype(jnp.bfloat16).astype(jnp.float32)
        rest = value - high
        middle = rest.astype(jnp.bfloat16).astype(jnp.float32)
        row = lax.broadcasted_iota(jnp.int32, (HD, rows), 0)
        parts = jnp.where(row == docs, high, jnp.where(row == docs + 1, middle, rest - middle))
        return jnp.where((row >= docs) & (row < docs + 3), parts, 0.0).astype(jnp.bfloat16)

    for source in range(4):
        span = slice(source * rows, (source + 1) * rows)
        for x in range(group):
            norm = stat_recv[source, x : x + 1, :] * (-1.0 / scale)
            qt_buf[x, 0, HD : 2 * HD, span] = query_marks[:, span] + three_parts(norm)
            qt_buf[x, 1, HD : 2 * HD, span] = three_parts(-stat_recv[source, 8 + x : 9 + x, :])

    def dot(left, right):
        return jnp.dot(left, right, preferred_element_type=jnp.float32)

    def beside(left, right):
        return jnp.concatenate([left, right], axis=1)

    def weigh(k, other, x, i0, j0, jn, diagonal_from=None):
        seen = slice(i0, i0 + wide)
        held = slice(j0, j0 + jn)
        marks = key_marks[k, other, held, :]
        scores = dot(beside(kv_buf[k, other, 0, held, :], marks), qt_buf[x, 0, :, seen])
        weight_grads = dot(beside(kv_buf[k, other, 1, held, :], marks), qt_buf[x, 1, :, seen])
        weights = jnp.exp(scores * scale)
        if diagonal_from is not None:
            key_places = lax.broadcasted_iota(jnp.int32, (wide, wide), 0)
            query_places = lax.broadcasted_iota(jnp.int32, (wide, wide), 1)
            cut = diagonal_from - j0
            later = jnp.where(key_places <= query_places, weights[cut : cut + wide], 0.0)
            weights = jnp.concatenate([weights[0:cut], later], axis=0) if cut else later
        score_grads = weights * weight_grads
        return weights.astype(jnp.bfloat16), score_grads.astype(jnp.bfloat16)

    def rows_of(x, part, first, end):
        return qd_buf[part, first:end, columns(x * HD)]

    def whole_tile(k, other, x):
        weights_a, grads_a = weigh(k, other, x, 0, 0, unit)
        weights_b, grads_b = weigh(k, other, x, wide, 0, unit)
        grads = beside(grads_a, grads_b)
        value_part = dot(beside(weights_a, weights_b), rows_of(x, 1, 0, unit))
        key_part = dot(grads, rows_of(x, 0, 0, unit))
        query_part = dot(kt_buf[k, other], grads)
        acc_kv[k, other, 1] += value_part
        acc_kv[k, other, 0] += key_part
        acc_q[x] += query_part

    def lower_tile(k, other, x, diagonal):
        weights_a, grads_a = weigh(k, other, x, 0, 0, wide, 0 if diagonal else None)
        weights_b, grads_b = weigh(k, other, x, wide, 0, unit, wide if diagonal else None)
        for part, a, b in ((1, weights_a, weights_b), (0, grads_a, grads_b)):
            acc_kv[k, other, part, 0:wide, :] += dot(beside(a, b[0:wide]), rows_of(x, part, 0, unit))
            acc_kv[k, other, part, wide:unit, :] += dot(
                b[wide:unit], rows_of(x, part, wide, unit)
            )
        acc_q[x, :, 0:wide] += dot(kt_buf[k, other, :, 0:wide], grads_a)
        acc_q[x, :, wide:unit] += dot(kt_buf[k, other], grads_b)

    def upper_tile(k, other, x):
        weights_a, grads_a = weigh(k, other, x, 0, 0, unit)
        weights_b, grads_b = weigh(k, other, x, wide, wide, wide)
        for part, a, b in ((1, weights_a, weights_b), (0, grads_a, grads_b)):
            acc_kv[k, other, part, 0:wide, :] += dot(a[0:wide], rows_of(x, part, 0, wide))
            acc_kv[k, other, part, wide:unit, :] += dot(beside(a[wide:unit], b), rows_of(x, part, 0, unit))
        acc_q[x, :, 0:wide] += dot(kt_buf[k, other], grads_a)
        acc_q[x, :, wide:unit] += dot(kt_buf[k, other, :, wide:unit], grads_b)

    def corner_tile(k, other, x, i0, j0):
        weights, grads = weigh(k, other, x, i0, j0, wide)
        seen, held = slice(i0, i0 + wide), slice(j0, j0 + wide)
        acc_kv[k, other, 1, held, :] += dot(weights, rows_of(x, 1, i0, i0 + wide))
        acc_kv[k, other, 0, held, :] += dot(grads, rows_of(x, 0, i0, i0 + wide))
        acc_q[x, :, seen] += dot(kt_buf[k, other, :, held], grads)

    def give(k, other, slots, slot, sems, device):
        out_sem = grad_out_sem.at[k, other]
        copies = [
            remote(
                grad_send.at[k, other, part],
                slots.at[slot, part],
                out_sem,
                sems.at[slot, part],
                device,
            )
            for part in range(2)
        ]
        return Parts(copies, grad_send.at[k, other], out_sem)

    def round_grads(k, other):
        grad_send[k, other] = acc_kv[k, other].astype(jnp.bfloat16)

    def take(k, other, slots, slot, sems, parts=(0, 1)):
        for part in parts:
            arrived(slots.at[slot, part], sems.at[slot, part])
            acc_kv[k, other, part] += slots[slot, part].astype(jnp.float32)

    far_side_given = give(3, 1, y_recv, 2, y_sem, side_twin)
    far_side_given_core = give(3, 1, core_recv, 3, core_sem, core_twin)
    far_given = give(3, 0, z_recv, 1, z_sem, before_other)
    far_given_core = give(3, 0, core_recv, 2, core_sem, core_twin)
    near_given = give(1, 0, core_recv, 0, core_sem, core_twin)
    near_side_given = give(1, 1, core_recv, 1, core_sem, core_twin)
    middle_given = give(2, 0, z_recv, 0, z_sem, before_same)
    middle_side_given = give(2, 1, y_recv, 1, y_sem, side_twin)
    own_side_given = give(0, 1, y_recv, 0, y_sem, side_twin)

    def gather_back(src, dst, out_sem, in_sem):
        for slot in range(4):
            part = src.at[slot * rows : (slot + 1) * rows, :]
            owner = 2 * core + slot // 2

            @pl.when((place == owner) & (core == slot % 2))
            def _():
                pltpu.make_async_copy(part, dst, in_sem).start()

            @pl.when((place != owner) | (core != slot % 2))
            def _():
                remote(
                    part, dst, out_sem, in_sem, (ROW * plane + owner, 2 * side + slot % 2)
                ).start()

    early = batches[0][1]

    def far_side_tile(x):
        @pl.when(side == 0)
        def _():
            upper_tile(3, 1, x)

        @pl.when(side == 1)
        def _():
            corner_tile(3, 1, x, 0, wide)

    def near_side_tile(x):
        @pl.when(side == 0)
        def _():
            corner_tile(0, 1, x, wide, 0)

        @pl.when(side == 1)
        def _():
            lower_tile(0, 1, x, False)

    def finish_query(x):
        dq_send[:, columns(x * HD)] = (acc_q[x].T * scale).astype(jnp.bfloat16)

    def return_query(first, count):
        gather_back(
            dq_send.at[:, columns(first * HD, count * HD)],
            dq_ref.at[:, columns((place * group + first) * HD, count * HD)],
            result_out_sem.at[0],
            result_sem.at[0],
        )

    def wait_q(index):
        first, end = batches[index]
        arrived(qd_buf.at[:, :, first * HD : end * HD], q_sem.at[index])
        for x in range(first, end):
            for part in range(2):
                qt_buf[x, part, 0:HD, :] = qd_buf[part, :, x * HD : (x + 1) * HD].T

    def over_heads(tile, first=early, end=group):
        def step(x, carry):
            tile(x)
            return carry

        lax.fori_loop(first, end, step, 0)

    def early_heads(tile):
        over_heads(tile, 0, early)

    @pl.when(has_before)
    def _():
        wait_kv(
            2,
            0,
            (second_core & has_after, before_to_after),
            (None, before_to_side),
            (None, before_to_core),
        )

    wait_q(0)
    early_heads(lambda x: lower_tile(0, 0, x, True))
    hand_on(1)

    @pl.when(has(1))
    def _():
        wait_kv(1, 0)

    def early_same_unit(index, carry):
        k = 2 - index

        @pl.when(has(k))
        def _():
            early_heads(lambda x: whole_tile(k, 0, x))

        return carry

    lax.fori_loop(0, 2, early_same_unit, 0)
    wait_kv(0, 1, (first_core, side_to_core))

    @pl.when(has(3))
    def _():
        wait_kv(3, 0, (first_core, far_to_side))
        early_heads(lambda x: upper_tile(3, 0, x))

    early_heads(near_side_tile)

    @pl.when(has_before)
    def _():
        wait_kv(2, 1, (None, before_side_to_core))

    @pl.when(has(1))
    def _():
        wait_kv(1, 1)

    def early_other_unit(index, carry):
        k = 2 - index

        @pl.when(has(k))
        def _():
            early_heads(lambda x: whole_tile(k, 1, x))

        return carry

    lax.fori_loop(0, 2, early_other_unit, 0)

    @pl.when(has(3))
    def _():
        wait_kv(3, 1)
        early_heads(far_side_tile)

    for x in range(early):
        finish_query(x)
    return_query(0, early)
    wait_q(1)

    @pl.when(has(3))
    def _():
        over_heads(far_side_tile)
        round_grads(3, 1)
        pl.when(first_core)(far_side_given.start)
        pl.when(second_core)(far_side_given_core.start)

    def other_unit(index, carry):
        k = 1 + index

        @pl.when(has(k))
        def _():
            over_heads(lambda x: whole_tile(k, 1, x))

        @pl.when((index == 0) & has(1))
        def _():
            round_grads(1, 1)
            near_side_given.start()

        return carry

    lax.fori_loop(0, 2, other_unit, 0)

    @pl.when(has_before)
    def _():
        take(2, 1, core_recv, 3 - 2 * core, core_sem)
        round_grads(2, 1)
        middle_side_given.start()

    @pl.when(has(3))
    def _():
        over_heads(lambda x: upper_tile(3, 0, x))

        @pl.when(first_core)
        def _():
            take(3, 0, y_recv, 2, y_sem)

        round_grads(3, 0)
        pl.when(first_core)(far_given.start)
        pl.when(second_core)(far_given_core.start)

    over_heads(near_side_tile)

    @pl.when(first_core)
    def _():
        take(0, 1, core_recv, 1, core_sem)

    round_grads(0, 1)
    own_side_given.start()

    def same_unit(index, carry):
        k = 1 + index

        @pl.when(has(k))
        def _():
            over_heads(lambda x: whole_tile(k, 0, x))

        @pl.when((index == 0) & has(1))
        def _():
            round_grads(1, 0)
            near_given.start()

        return carry

    lax.fori_loop(0, 2, same_unit, 0)

    @pl.when(has_before)
    def _():
        take(2, 0, core_recv, 2 - 2 * core, core_sem)
        take(2, 0, y_recv, 1, y_sem)

        @pl.when(second_core & has_after)
        def _():
            take(2, 0, z_recv, 1, z_sem)

        round_grads(2, 0)
        middle_given.start()

    def own_head(x):
        lower_tile(0, 0, x, True)
        finish_query(x)
        return_query(x, 1)

    over_heads(own_head)

    for part, ref, factor in ((0, dk_ref, scale), (1, dv_ref, 1.0)):

        @pl.when(first_core)
        def _():
            take(0, 0, core_recv, 0, core_sem, (part,))

        take(0, 0, y_recv, 0, y_sem, (part,))

        @pl.when(has_after)
        def _():
            take(0, 0, z_recv, 0, z_sem, (part,))

        dkv_send[part] = (acc_kv[0, 0, part] * factor).astype(jnp.bfloat16)
        gather_back(
            dkv_send.at[part],
            ref.at[:, columns(place * HD)],
            result_out_sem.at[1 + part],
            result_sem.at[1 + part],
        )

    def drain(away):
        arrived(kv_buf.at[0, 0, :, 0:away, :], kv_in_out_sem.at[0])
        arrived(qd_buf.at[0, 0:away, :], q_out_sem.at[0])
        arrived(qd_buf.at[1, 0 : away - rows, :], q_out_sem.at[1])
        arrived(stat_recv.at[0 : away // rows], stat_sem.at[0])

    @pl.when(stays)
    def _():
        drain(unit - rows)

    @pl.when(jnp.logical_not(stays))
    def _():
        drain(unit)

    for index, (x, end) in enumerate(batches):
        arrived(relay_buf.at[:, x * HD : end * HD], relay_sem.at[2, index])
        to_between[index].wait_send()
    own_to_side.wait_send()
    own_side_given.wait_send()

    @pl.when(has_after)
    def _():
        own_to_after.wait_send()

    @pl.when(first_core)
    def _():
        own_to_core.wait_send()
        side_to_core.wait_send()

    @pl.when(has_before)
    def _():
        before_to_side.wait_send()
        before_to_core.wait_send()
        before_side_to_core.wait_send()
        middle_given.wait_send()
        middle_side_given.wait_send()

    @pl.when(second_core & has_before & has_after)
    def _():
        before_to_after.wait_send()

    @pl.when(has(1))
    def _():
        near_given.wait_send()
        near_side_given.wait_send()

    @pl.when(has(3))
    def _():
        far_given.wait_send()
        far_side_given.wait_send()

        @pl.when(first_core)
        def _():
            far_to_side.wait_send()

    def drain_back(away):
        arrived(dq_send.at[0:away, :], result_out_sem.at[0])
        for part in range(2):
            arrived(dkv_send.at[part, 0:away, :], result_out_sem.at[1 + part])

    @pl.when(stays)
    def _():
        drain_back(unit - rows)

    @pl.when(jnp.logical_not(stays))
    def _():
        drain_back(unit)

    for index, ref in enumerate((dq_ref, dk_ref, dv_ref)):
        arrived(ref, result_sem.at[index])


def hand_over(dq_in, dk_in, dv_in, dq_out, dk_out, dv_out, dq_vm, dk_vm, dv_vm, sems):
    ways = ((dk_in, dk_vm, dk_out), (dv_in, dv_vm, dv_out), (dq_in, dq_vm, dq_out))
    ins = [pltpu.make_async_copy(src, vm, sems.at[0, i]) for i, (src, vm, dst) in enumerate(ways)]
    outs = [pltpu.make_async_copy(vm, dst, sems.at[1, i]) for i, (src, vm, dst) in enumerate(ways)]
    for copy in ins:
        copy.start()
    for first, second in zip(ins, outs):
        first.wait()
        second.start()
    for copy in outs:
        copy.wait()


def body(queries, keys, values, attn_out, grad_out, log_norm, doc_lengths):
    heads = lax.axis_size("head")
    planes = lax.axis_size("ctx") // ROW
    rows = queries.shape[0]
    unit = rows * heads
    group = queries.shape[1] // keys.shape[1]
    low, full = jnp.bfloat16, jnp.float32
    anywhere = pl.BlockSpec(memory_space=pl.ANY)
    pairs = unit * unit * 6.5 * group
    dma = pltpu.SemaphoreType.DMA
    results = (
        jax.ShapeDtypeStruct(queries.shape, low),
        jax.ShapeDtypeStruct(keys.shape, low),
        jax.ShapeDtypeStruct(values.shape, low),
    )
    gradients = pl.pallas_call(
        functools.partial(kernel, planes, group),
        out_shape=results,
        in_specs=[pl.BlockSpec(memory_space=pltpu.SMEM)]
        + [anywhere] * 5
        + [pl.BlockSpec(memory_space=pltpu.VMEM)],
        out_specs=(anywhere, anywhere, anywhere),
        scratch_shapes=[
            pltpu.VMEM(attn_out.shape, low),
            pltpu.VMEM(grad_out.shape, low),
            pltpu.VMEM((2, unit, group * HD), low),
            pltpu.VMEM((rows, group * HD), low),
            pltpu.VMEM((group, 2, 2 * HD, unit), low),
            pltpu.VMEM((BACK + 1, 2, 2, unit, HD), low),
            pltpu.VMEM((BACK + 1, 2, HD, unit), low),
            pltpu.VMEM((ROW, 16, rows), full),
            pltpu.VMEM((4, 16, rows), full),
            pltpu.VMEM((HD, unit), full),
            pltpu.VMEM((BACK + 1, 2, unit, HD), low),
            pltpu.VMEM((BACK + 1, 2, 2, unit, HD), full),
            pltpu.VMEM((group, HD, unit), full),
            pltpu.VMEM((BACK + 1, 2, 2, unit, HD), low),
            pltpu.VMEM((4, 2, unit, HD), low),
            pltpu.VMEM((3, 2, unit, HD), low),
            pltpu.VMEM((2, 2, unit, HD), low),
            pltpu.VMEM((unit, group * HD), low),
            pltpu.VMEM((2, unit, HD), low),
            dma((2,)),
            dma((2,)),
            dma((2,)),
            dma((3, 2)),
            dma((BACK + 1, 2, 2)),
            dma((1,)),
            dma((9,)),
            dma((2,)),
            dma((4, 2)),
            dma((3, 2)),
            dma((2, 2)),
            dma((BACK + 1, 2)),
            dma((3,)),
            dma((3,)),
        ],
        compiler_params=pltpu.CompilerParams(
            collective_id=0, has_side_effects=True, vmem_limit_bytes=63 * 1024 * 1024
        ),
        cost_estimate=pl.CostEstimate(
            flops=int(10 * pairs * HD), bytes_accessed=8 * 1024 * 1024, transcendentals=int(pairs)
        ),
    )(doc_lengths, queries, keys, values, attn_out, grad_out, log_norm)
    return pl.pallas_call(
        hand_over,
        out_shape=results,
        in_specs=[anywhere] * 3,
        out_specs=(anywhere,) * 3,
        scratch_shapes=[pltpu.VMEM(result.shape, low) for result in results] + [dma((2, 3))],
        compiler_params=pltpu.CompilerParams(vmem_limit_bytes=63 * 1024 * 1024),
        cost_estimate=pl.CostEstimate(flops=0, bytes_accessed=2 * 1024 * 1024, transcendentals=0),
    )(*gradients)


def solution(mesh):
    spread = P(("ctx", "head"), None)
    return jax.shard_map(
        body,
        mesh=mesh,
        in_specs=(spread, spread, spread, spread, spread, P(None, ("ctx", "head")), P()),
        out_specs=(spread, spread, spread),
        check_vma=False,
    )
```

time: 313 us -> 73.9 us (0.24)
  the two profiles are of different devices: /device:TPU:86 before, /device:TPU:217 now
where the time goes in v1:
time: 73.9 us; the launch traced here: 73.7 us
  Pallas kernels  73.1 us (99%)
    pallas_call x1, Pallas kernels, body(): pl.pallas_call(functools.partial(kernel, planes, group), out_shape=result...  71 us
    pallas_call x1, Pallas kernels, body(): pl.pallas_call(hand_over, out_shape=results, in_specs=[anywhere] * 3, out...  2.11 us

profile of v1, /device:TPU:217, one launch (start us, length us, event | category | flops | bytes accessed | tf_op | source)
XLA Modules:
  0.0 73.7 jit_solution(16859580708872594847)
XLA Ops:
  0.6 71.0 %shard_map.94 = (bf16[128,2560]{1,0:T(8,128)(2,1)}, bf16[128,512]{1,0:T(8,128)(2,1)}, bf16[128,512]{1,0:T(8,128)(2,1)}) custom-call(s32[64]{0:T(128)} %docs_ref.1, bf16[128,2560]{1,0:T(8,128)(2,1)} %q_ref.1, bf16[128,512]{1,0:T(8,128)(2,1)} %k_ref.1, bf16[128,512]{1,0:T(8,128)(2,1)} %v_ref.1, bf16[128,2560]{1,0:T(8,128)(2,1)} %o_ref.1, ...), custom_call_target="tpu_custom_call" | custom-call | flops 10905190400 | bytes 8388608 | tf_op jit(solution)/shard_map/pallas_call | solution.py:755
  71.6 2.1 %shard_map.95 = (bf16[128,2560]{1,0:T(8,128)(2,1)}, bf16[128,512]{1,0:T(8,128)(2,1)}, bf16[128,512]{1,0:T(8,128)(2,1)}) custom-call(bf16[128,2560]{1,0:T(8,128)(2,1)} %get-tuple-element.6.dq_in, bf16[128,512]{1,0:T(8,128)(2,1)} %get-tuple-element.7.dk_in, bf16[128,512]{1,0:T(8,128)(2,1)} %get-tuple-element.8.dv_in), custom_call_target="tpu_custom_call" | custom-call | bytes 2097152 | tf_op jit(solution)/shard_map/pallas_call | solution.py:804

commit v2 on v1

--- a/solution.py
+++ b/solution.py
@@ -472,11 +472,8 @@
                 qt_buf[x, part, 0:HD, :] = qd_buf[part, :, x * HD : (x + 1) * HD].T
 
     def over_heads(tile, first=early, end=group):
-        def step(x, carry):
+        for x in range(first, end):
             tile(x)
-            return carry
-
-        lax.fori_loop(first, end, step, 0)
 
     def early_heads(tile):
         over_heads(tile, 0, early)

time: 73.9 us -> 74.4 us (level); the launches traced: 73.7 us -> 73.3 us
  no operation moved by 1% of the time
where the time goes in v2:
time: 74.4 us; the launch traced here: 73.3 us
  Pallas kernels  72.5 us (97%)
  between operations  0.8 us (1%)
    pallas_call x1, Pallas kernels, body(): pl.pallas_call(functools.partial(kernel, planes, group), out_shape=result...  70.3 us
    pallas_call x1, Pallas kernels, body(): pl.pallas_call(hand_over, out_shape=results, in_specs=[anywhere] * 3, out...  2.11 us

profile of v2, /device:TPU:217, one launch (start us, length us, event | category | flops | bytes accessed | tf_op | source)
XLA Modules:
  0.0 73.3 jit_solution(1604042996820373712)
XLA Ops:
  0.6 70.3 %shard_map.94 = (bf16[128,2560]{1,0:T(8,128)(2,1)}, bf16[128,512]{1,0:T(8,128)(2,1)}, bf16[128,512]{1,0:T(8,128)(2,1)}) custom-call(s32[64]{0:T(128)} %docs_ref.1, bf16[128,2560]{1,0:T(8,128)(2,1)} %q_ref.1, bf16[128,512]{1,0:T(8,128)(2,1)} %k_ref.1, bf16[128,512]{1,0:T(8,128)(2,1)} %v_ref.1, bf16[128,2560]{1,0:T(8,128)(2,1)} %o_ref.1, ...), custom_call_target="tpu_custom_call" | custom-call | flops 10905190400 | bytes 8388608 | tf_op jit(solution)/shard_map/pallas_call | solution.py:752
  71.0 2.1 %shard_map.95 = (bf16[128,2560]{1,0:T(8,128)(2,1)}, bf16[128,512]{1,0:T(8,128)(2,1)}, bf16[128,512]{1,0:T(8,128)(2,1)}) custom-call(bf16[128,2560]{1,0:T(8,128)(2,1)} %get-tuple-element.6.dq_in, bf16[128,512]{1,0:T(8,128)(2,1)} %get-tuple-element.7.dk_in, bf16[128,512]{1,0:T(8,128)(2,1)} %get-tuple-element.8.dv_in), custom_call_target="tpu_custom_call" | custom-call | bytes 2097152 | tf_op jit(solution)/shard_map/pallas_call | solution.py:801
